TPU v7x, 32 devices: a whole 2x2x4 slice. The times are simulated.
32 devices in a mesh: section: 4 (over x, core), expert: 2 (over y), dp: 4 (over z).
Axes of the slice: x: 2, y: 2, z: 4, core: 2. Of those that a mesh axis runs over, the one named last changes fastest.
Arguments:
- in_flight: bfloat16 [4, 2, 128, 3584], P('section', None, 'expert', 'dp'), may hold values from -6 to 6
- incoming: bfloat16 [2, 128, 3584], P(None, 'expert', 'dp'), may hold values from -6 to 6
- up_proj: bfloat16 [4, 32, 3584, 1152], P('section', 'expert', 'dp'), may hold values from -0.09375 to 0.09375
- down_proj: bfloat16 [4, 32, 1152, 3584], P('section', 'expert', None, 'dp'), may hold values from -0.1875 to 0.1875
- expert_ids: int32 [2, 4, 2, 128, 4], P(None, 'section', None, 'expert'), may hold values from 0 to 31, all different within a row; in each aligned block of 64 rows (0 to 63, 64 to 127, ..., all dimensions but the last counted through in order) at most 12 rows name the same one
- gate_logits: float32 [2, 4, 2, 128, 4], P(None, 'section', None, 'expert'), may hold values from -6 to 6
Outputs:
- states: bfloat16 [2, 4, 2, 128, 3584], P(None, 'section', None, 'expert', 'dp')
Inputs may be any that keep to these rules, and one draw needn't show every extreme that they name: `expert_ids`: each row names 4 different experts. In every aligned block of 64 rows, no expert is named by more than 12 rows, a bound that some block reaches.
All inputs are finite; a program needn't handle non-finite values.
Results may differ from a plain program's by a relative error of at most 0.015.
Values may be sent and summed in bfloat16 or wider, within the bound.
A program may use at most 192 MiB of HBM per device.

v0:
```python
import jax
import jax.numpy as jnp
from jax import lax
from jax.sharding import PartitionSpec as P

MB = 2
TICKS = 2
TOP = 4


def shifted(block, axis, distance):
    devices = range(lax.axis_size(axis))
    route = [(i - distance, i) for i in devices if i - distance in devices]
    return lax.ppermute(block, axis, route)


def gate_weights(logits):
    squashed = jax.nn.sigmoid(logits)
    return 2.5 * squashed / jnp.sum(squashed, axis=-1, keepdims=True)


def routing_slots(routing, experts, capacity):
    pair_ids = routing.reshape(-1)
    onehot = (pair_ids[:, None] == jnp.arange(experts, dtype=jnp.int32)[None, :]).astype(jnp.int32)
    before = jnp.cumsum(onehot, axis=0) - onehot
    slot_numbers = jnp.sum(before * onehot, axis=1)
    return pair_ids * capacity + slot_numbers


def experts_layer(tokens_in, routing, logits, up_weight, down_weight, capacity):
    batch_count, row_count, feature_width = tokens_in.shape
    per_device = up_weight.shape[0]
    groups = lax.axis_size("expert")
    experts = per_device * groups
    slots_total = experts * capacity
    slot_block = per_device * capacity
    flats = jnp.stack([routing_slots(routing[0], experts, capacity)])
    row_ids = jnp.broadcast_to(
        jnp.arange(row_count, dtype=jnp.int32)[:, None], (row_count, TOP)
    ).reshape(-1)

    def fill_table(slot_index):
        return jnp.full((slots_total,), -1, jnp.int32).at[slot_index].set(row_ids)

    sources = jax.vmap(fill_table)(flats)
    offset = jnp.arange(batch_count, dtype=jnp.int32)[:, None] * row_count
    source_index = jnp.where(sources >= 0, sources + offset, -1)
    source_index = (
        source_index.reshape(batch_count, groups, slot_block).transpose(1, 0, 2).reshape(-1)
    )
    flat_tokens = tokens_in.reshape(batch_count * row_count, feature_width)
    outgoing = jnp.where(
        (source_index >= 0)[:, None],
        flat_tokens[jnp.maximum(source_index, 0)],
        jnp.zeros((), flat_tokens.dtype),
    )
    outgoing = outgoing.reshape(groups, batch_count, per_device, capacity, feature_width)
    arrived = lax.all_to_all(outgoing, "expert", split_axis=0, concat_axis=0, tiled=True)
    partial_value = jnp.einsum(
        "gmxcd,xdf->gmxcf", arrived, up_weight, preferred_element_type=jnp.float32
    )
    rounded = lax.optimization_barrier(partial_value.astype(jnp.bfloat16)).astype(jnp.float32)
    summed = lax.psum(rounded.astype(jnp.bfloat16), "dp").astype(jnp.float32)
    hidden = jax.nn.silu(summed).astype(jnp.bfloat16)
    produced = jnp.einsum(
        "gmxcf,xfd->gmxcd", hidden, down_weight, preferred_element_type=jnp.float32
    ).astype(jnp.bfloat16)
    returned = lax.all_to_all(produced, "expert", split_axis=0, concat_axis=0, tiled=True)
    pick_index = (
        flats // slot_block * (batch_count * slot_block)
        + jnp.arange(batch_count, dtype=jnp.int32)[:, None] * slot_block
        + flats % slot_block
    )
    gathered = returned.reshape(-1, feature_width)[pick_index.reshape(-1)].reshape(
        batch_count, row_count, TOP, feature_width
    )
    weights = gate_weights(logits)
    routed_sum = jnp.einsum("mrk,mrkd->mrd", weights, gathered.astype(jnp.float32))
    return (tokens_in.astype(jnp.float32) + routed_sum).astype(jnp.bfloat16)


def body(in_flight, incoming, up_proj, down_proj, expert_ids, gate_logits):
    up_weight = up_proj[0]
    down_weight = down_proj[0]
    groups = lax.axis_size("expert")
    row_count = in_flight.shape[2]
    per_device = up_weight.shape[0]
    capacity = max(2, 3 * row_count * TOP // (2 * per_device * groups))
    current = in_flight[0]
    is_first = lax.axis_index("section") == 0
    states = []
    for tick_index in range(TICKS):
        if tick_index > 0:
            handed_on = shifted(states[-1], "section", 1)
            current = jnp.where(is_first, incoming, handed_on)
        routing = expert_ids[tick_index, 0]
        logits = gate_logits[tick_index, 0]
        pieces = [
            experts_layer(
                current[micro_index : micro_index + 1],
                routing[micro_index : micro_index + 1],
                logits[micro_index : micro_index + 1],
                up_weight,
                down_weight,
                capacity,
            )
            for micro_index in range(MB)
        ]
        result = jnp.concatenate(pieces, axis=0)
        states.append(result)
    return jnp.stack(states)[:, None]


def solution(mesh):
    return jax.shard_map(
        body,
        mesh=mesh,
        in_specs=(
            P("section", None, "expert", "dp"),
            P(None, "expert", "dp"),
            P("section", "expert", "dp", None),
            P("section", "expert", None, "dp"),
            P(None, "section", None, "expert", None),
            P(None, "section", None, "expert", None),
        ),
        out_specs=P(None, "section", None, "expert", "dp"),
        check_vma=False,
    )
```

profile of v0, /device:TPU:0, one launch (start us, length us, event | category | flops | bytes accessed | tf_op | source)
XLA Modules:
  0.0 419.1 jit_solution(6437509623442721821)
XLA Ops:
  6.5 0.7 fusion.147
  8.9 1.4 scatter_custom_fusion
  10.3 1.0 slice_bitcast_fusion.1
  11.3 2.3 gather_fusion
  14.1 1.0 copy.45
  15.1 4.2 %all-to-all-start = ((bf16[2,1,16,12,896]{4,2,3,1,0:T(8,128)(2,1)}), bf16[2,1,16,12,896]{4,2,3,1,0:T(8,128)(2,1)S(1)}, u32[]{:S(2)}, u32[]{:S(2)}) async-start(bf16[2,1,16,12,896]{4,2,3,1,0:T(8,128)(2,1)} %copy.45), calls=%async_computation | async-start | bytes 1376256 | tf_op jit(solution)/shard_map/all_to_all | solution.py:58
  19.6 0.6 reduce-window.30
  20.8 1.4 scatter_custom_fusion.1
  22.2 2.3 gather_fusion.2
  25.7 1.0 copy.54
  27.7 0.6 reduce-window.36
  28.3 1.5 all-to-all-done
  29.8 3.5 all-to-all-start.2
  33.9 14.3 %fusion.37 = bf16[2,1,16,12,1152]{4,3,0,2,1:T(8,128)(2,1)} fusion(bf16[1,16,896,1152]{3,2,1,0:T(8,128)(2,1)} %param.8, bf16[2,1,16,12,896]{4,2,3,1,0:T(8,128)(2,1)S(1)} %all-to-all-done), kind=kOutput, calls=%fused_computation.43 | convolution fusion | flops 793165824 | bytes 34603008 | tf_op jit(solution)/shard_map/gmxcd,xdf->gmxcf/dot_general | solution.py:59
  48.2 14.3 %fusion.34 = bf16[2,1,16,12,1152]{4,3,0,2,1:T(8,128)(2,1)} fusion(bf16[1,16,896,1152]{3,2,1,0:T(8,128)(2,1)} %param.8, bf16[2,1,16,12,896]{4,2,3,1,0:T(8,128)(2,1)S(1)} %all-to-all-done.2), kind=kOutput, calls=%fused_computation.42 | convolution fusion | flops 793165824 | bytes 34603008 | tf_op jit(solution)/shard_map/gmxcd,xdf->gmxcf/dot_general | solution.py:59
  63.5 97.1 %all-reduce.7.cloned.1.call-done = (bf16[2,1,16,12,1152]{4,3,0,2,1:T(8,128)(2,1)}, bf16[2,1,16,12,1152]{4,3,0,2,1:T(8,128)(2,1)}) async-done(((bf16[2,1,16,12,1152]{4,3,0,2,1:T(8,128)(2,1)}, bf16[2,1,16,12,1152]{4,3,0,2,1:T(8,128)(2,1)}), (bf16[2,1,16,12,1152]{4,3,0,2,1:T(8,128)(2,1)}, bf16[2,1,16,12,1152]{4,3,0,2,1:T(8,128)(2,1)})) %all-reduce.7.cloned.1.call-update) | async-done | bytes 1769488 | tf_op jit(solution)/shard_map/psum | solution.py:63
  160.6 15.8 %fusion.74 = bf16[2,1,16,12,896]{4,3,0,2,1:T(8,128)(2,1)S(1)} fusion(bf16[1,16,1152,896]{3,2,1,0:T(8,128)(2,1)} %param.9, bf16[2,1,16,12,1152]{4,3,0,2,1:T(8,128)(2,1)} %get-tuple-element.11), kind=kOutput, calls=%fused_computation.66 | convolution fusion | flops 795721728 | bytes 34603008 | tf_op jit(solution)/shard_map/gmxcf,xfd->gmxcd/dot_general | solution.py:65
  176.4 1.1 copy.56
  177.5 3.5 all-to-all-start.3
  181.0 12.5 %fusion.77 = bf16[2,1,16,12,896]{4,3,0,2,1:T(8,128)(2,1)S(1)} fusion(bf16[1,16,1152,896]{3,2,1,0:T(8,128)(2,1)} %param.9, bf16[2,1,16,12,1152]{4,3,0,2,1:T(8,128)(2,1)S(1)} %copy-done), kind=kOutput, calls=%fused_computation.67 | convolution fusion | flops 795721728 | bytes 34603008 | tf_op jit(solution)/shard_map/gmxcf,xfd->gmxcd/dot_general | solution.py:65
  193.5 1.1 copy.47
  194.6 3.5 all-to-all-start.1
  198.5 1.6 scatter_custom_fusion.2
  200.6 1.2 gather_fusion.3
  201.9 6.2 %all-to-all-done.1 = bf16[2,1,16,12,896]{4,2,3,1,0:T(8,128)(2,1)S(1)} async-done(((bf16[2,1,16,12,896]{4,2,3,1,0:T(8,128)(2,1)}), bf16[2,1,16,12,896]{4,2,3,1,0:T(8,128)(2,1)S(1)}, u32[]{:S(2)}, u32[]{:S(2)}) %all-to-all-start.1) | async-done | bytes 688160 | tf_op jit(solution)/shard_map/all_to_all | solution.py:68
  208.4 1.2 gather_fusion.1
  210.7 1.3 collective-permute-start
  212.0 1.4 scatter_custom_fusion.3
  213.7 2.3 gather_fusion.4
  216.3 1.0 copy.63
  217.3 3.5 all-to-all-start.4
  220.8 2.3 gather_fusion.6
  223.5 1.0 copy.72
  224.5 4.9 %all-to-all-done.4 = bf16[2,1,16,12,896]{4,2,3,1,0:T(8,128)(2,1)S(1)} async-done(((bf16[2,1,16,12,896]{4,2,3,1,0:T(8,128)(2,1)}), bf16[2,1,16,12,896]{4,2,3,1,0:T(8,128)(2,1)S(1)}, u32[]{:S(2)}, u32[]{:S(2)}) %all-to-all-start.4) | async-done | bytes 688160 | tf_op jit(solution)/shard_map/all_to_all | solution.py:58
  229.4 3.5 all-to-all-start.6
  233.2 14.3 %fusion.31 = bf16[2,1,16,12,1152]{4,3,0,2,1:T(8,128)(2,1)} fusion(bf16[1,16,896,1152]{3,2,1,0:T(8,128)(2,1)} %param.8, bf16[2,1,16,12,896]{4,2,3,1,0:T(8,128)(2,1)S(1)} %all-to-all-done.4), kind=kOutput, calls=%fused_computation.41 | convolution fusion | flops 793165824 | bytes 34603008 | tf_op jit(solution)/shard_map/gmxcd,xdf->gmxcf/dot_general | solution.py:59
  247.5 14.2 %fusion.28 = bf16[2,1,16,12,1152]{4,3,0,2,1:T(8,128)(2,1)} fusion(bf16[1,16,896,1152]{3,2,1,0:T(8,128)(2,1)} %param.8, bf16[2,1,16,12,896]{4,2,3,1,0:T(8,128)(2,1)S(1)} %all-to-all-done.6), kind=kOutput, calls=%fused_computation.40 | convolution fusion | flops 793165824 | bytes 34603008 | tf_op jit(solution)/shard_map/gmxcd,xdf->gmxcf/dot_general | solution.py:59
  261.8 99.0 %all-reduce.5.cloned.1.call-done = (bf16[2,1,16,12,1152]{4,3,0,2,1:T(8,128)(2,1)}, bf16[2,1,16,12,1152]{4,3,0,2,1:T(8,128)(2,1)}) async-done(((bf16[2,1,16,12,1152]{4,3,0,2,1:T(8,128)(2,1)}, bf16[2,1,16,12,1152]{4,3,0,2,1:T(8,128)(2,1)}), (bf16[2,1,16,12,1152]{4,3,0,2,1:T(8,128)(2,1)}, bf16[2,1,16,12,1152]{4,3,0,2,1:T(8,128)(2,1)})) %all-reduce.5.cloned.1.call-update) | async-done | bytes 1769488 | tf_op jit(solution)/shard_map/psum | solution.py:63
  360.8 15.8 %fusion.68 = bf16[2,1,16,12,896]{4,3,0,2,1:T(8,128)(2,1)S(1)} fusion(bf16[1,16,1152,896]{3,2,1,0:T(8,128)(2,1)} %param.9, bf16[2,1,16,12,1152]{4,3,0,2,1:T(8,128)(2,1)} %get-tuple-element.9), kind=kOutput, calls=%fused_computation.64 | convolution fusion | flops 795721728 | bytes 34603008 | tf_op jit(solution)/shard_map/gmxcf,xfd->gmxcd/dot_general | solution.py:65
  376.7 1.1 copy.74
  377.8 3.5 all-to-all-start.7
  381.3 12.5 %fusion.71 = bf16[2,1,16,12,896]{4,3,0,2,1:T(8,128)(2,1)S(1)} fusion(bf16[1,16,1152,896]{3,2,1,0:T(8,128)(2,1)} %param.9, bf16[2,1,16,12,1152]{4,3,0,2,1:T(8,128)(2,1)S(1)} %copy-done.1), kind=kOutput, calls=%fused_computation.65 | convolution fusion | flops 795721728 | bytes 34603008 | tf_op jit(solution)/shard_map/gmxcf,xfd->gmxcd/dot_general | solution.py:65
  393.8 1.1 copy.65
  394.9 3.8 all-to-all-start.5
  399.4 1.2 gather_fusion.7
  400.7 7.9 %all-to-all-done.5 = bf16[2,1,16,12,896]{4,2,3,1,0:T(8,128)(2,1)S(1)} async-done(((bf16[2,1,16,12,896]{4,2,3,1,0:T(8,128)(2,1)}), bf16[2,1,16,12,896]{4,2,3,1,0:T(8,128)(2,1)S(1)}, u32[]{:S(2)}, u32[]{:S(2)}) %all-to-all-start.5) | async-done | bytes 688160 | tf_op jit(solution)/shard_map/all_to_all | solution.py:68
  408.9 1.2 gather_fusion.5
  411.2 0.8 maximum_bitcast_fusion
  (142 shorter events, 12.3 us)
Async XLA Ops:
  15.1 14.7 %all-to-all-start = ((bf16[2,1,16,12,896]{4,2,3,1,0:T(8,128)(2,1)}), bf16[2,1,16,12,896]{4,2,3,1,0:T(8,128)(2,1)S(1)}, u32[]{:S(2)}, u32[]{:S(2)}) async-start(bf16[2,1,16,12,896]{4,2,3,1,0:T(8,128)(2,1)} %copy.45), calls=%async_computation | async-start | bytes 1376256 | tf_op jit(solution)/shard_map/all_to_all | solution.py:58
  27.5 20.7 %copy-start.5 = (s32[32,3]{0,1:T(4,128)}, s32[32,3]{0,1:T(4,128)S(1)}, u32[]{:S(2)}) copy-start(s32[32,3]{0,1:T(4,128)S(1)} %reduce-window.35) | copy-start | bytes 1156
  29.8 18.4 %all-to-all-start.2 = ((bf16[2,1,16,12,896]{4,2,3,1,0:T(8,128)(2,1)}), bf16[2,1,16,12,896]{4,2,3,1,0:T(8,128)(2,1)S(1)}, u32[]{:S(2)}, u32[]{:S(2)}) async-start(bf16[2,1,16,12,896]{4,2,3,1,0:T(8,128)(2,1)} %copy.54), calls=%async_computation.2 | async-start | bytes 1376256 | tf_op jit(solution)/shard_map/all_to_all | solution.py:58
  33.3 127.2 %all-reduce.7.cloned.1.call-start = ((), (), s32[]{:S(2)}) async-start(), calls=%async_computation.9 | async-start | bytes 4718592 | tf_op jit(solution)/shard_map/psum | solution.py:63
  62.5 0.7 slice-start
  62.5 0.8 copy-start.4
  176.4 4.6 %copy-start = (bf16[2,1,16,12,1152]{4,3,0,2,1:T(8,128)(2,1)S(1)}, bf16[2,1,16,12,1152]{4,3,0,2,1:T(8,128)(2,1)}, u32[]{:S(2)}) copy-start(bf16[2,1,16,12,1152]{4,3,0,2,1:T(8,128)(2,1)} %get-tuple-element.12) | copy-start | bytes 2654212
  177.5 17.1 %all-to-all-start.3 = ((bf16[2,1,16,12,896]{4,2,3,1,0:T(8,128)(2,1)}), bf16[2,1,16,12,896]{4,2,3,1,0:T(8,128)(2,1)S(1)}, u32[]{:S(2)}, u32[]{:S(2)}) async-start(bf16[2,1,16,12,896]{4,2,3,1,0:T(8,128)(2,1)} %copy.56), calls=%async_computation.3 | async-start | bytes 1376256 | tf_op jit(solution)/shard_map/all_to_all | solution.py:68
  194.6 13.5 %all-to-all-start.1 = ((bf16[2,1,16,12,896]{4,2,3,1,0:T(8,128)(2,1)}), bf16[2,1,16,12,896]{4,2,3,1,0:T(8,128)(2,1)S(1)}, u32[]{:S(2)}, u32[]{:S(2)}) async-start(bf16[2,1,16,12,896]{4,2,3,1,0:T(8,128)(2,1)} %copy.47), calls=%async_computation.1 | async-start | bytes 1376256 | tf_op jit(solution)/shard_map/all_to_all | solution.py:68
  209.6 1.0 copy-start.2
  209.6 4.0 copy-start.3
  210.7 2.9 collective-permute-start
  217.3 12.1 %all-to-all-start.4 = ((bf16[2,1,16,12,896]{4,2,3,1,0:T(8,128)(2,1)}), bf16[2,1,16,12,896]{4,2,3,1,0:T(8,128)(2,1)S(1)}, u32[]{:S(2)}, u32[]{:S(2)}) async-start(bf16[2,1,16,12,896]{4,2,3,1,0:T(8,128)(2,1)} %copy.63), calls=%async_computation.4 | async-start | bytes 1376256 | tf_op jit(solution)/shard_map/all_to_all | solution.py:58
  229.4 18.1 %all-to-all-start.6 = ((bf16[2,1,16,12,896]{4,2,3,1,0:T(8,128)(2,1)}), bf16[2,1,16,12,896]{4,2,3,1,0:T(8,128)(2,1)S(1)}, u32[]{:S(2)}, u32[]{:S(2)}) async-start(bf16[2,1,16,12,896]{4,2,3,1,0:T(8,128)(2,1)} %copy.72), calls=%async_computation.6 | async-start | bytes 1376256 | tf_op jit(solution)/shard_map/all_to_all | solution.py:58
  232.9 127.9 %all-reduce.5.cloned.1.call-start = ((), (), s32[]{:S(2)}) async-start(), calls=%async_computation.8 | async-start | bytes 4718592 | tf_op jit(solution)/shard_map/psum | solution.py:63
  376.6 4.6 %copy-start.1 = (bf16[2,1,16,12,1152]{4,3,0,2,1:T(8,128)(2,1)S(1)}, bf16[2,1,16,12,1152]{4,3,0,2,1:T(8,128)(2,1)}, u32[]{:S(2)}) copy-start(bf16[2,1,16,12,1152]{4,3,0,2,1:T(8,128)(2,1)} %get-tuple-element.10) | copy-start | bytes 2654212
  377.8 17.1 %all-to-all-start.7 = ((bf16[2,1,16,12,896]{4,2,3,1,0:T(8,128)(2,1)}), bf16[2,1,16,12,896]{4,2,3,1,0:T(8,128)(2,1)S(1)}, u32[]{:S(2)}, u32[]{:S(2)}) async-start(bf16[2,1,16,12,896]{4,2,3,1,0:T(8,128)(2,1)} %copy.74), calls=%async_computation.7 | async-start | bytes 1376256 | tf_op jit(solution)/shard_map/all_to_all | solution.py:68
  394.9 13.7 %all-to-all-start.5 = ((bf16[2,1,16,12,896]{4,2,3,1,0:T(8,128)(2,1)}), bf16[2,1,16,12,896]{4,2,3,1,0:T(8,128)(2,1)S(1)}, u32[]{:S(2)}, u32[]{:S(2)}) async-start(bf16[2,1,16,12,896]{4,2,3,1,0:T(8,128)(2,1)} %copy.65), calls=%async_computation.5 | async-start | bytes 1376256 | tf_op jit(solution)/shard_map/all_to_all | solution.py:68
Sparse Core Ops, SparseCore 0:
  62.6 97.9 all-reduce.6
  261.8 98.9 all-reduce.4
where the time goes:
time: 425 us; the launch traced here: 419 us
  waiting for transfers between devices  217 us (51%)
  matrix products  115 us (27%)
  local copies, waits for them, and re-layouts  35.6 us (8%)
  starting transfers between devices  31.2 us (7%)
  between operations  14.4 us (3%)
  other arithmetic  5.76 us (1%)
    psum x2, waiting for transfers between devices, experts_layer(): summed = lax.psum(rounded.astype(jnp.bfloat16), 'dp').astype(jnp.float32)  196 us
    dot_general x4, matrix products, experts_layer(): jnp.einsum('gmxcd,xdf->gmxcf', arrived, up_weight, preferred_element_type...  57.1 us
    dot_general x4, matrix products, experts_layer(): jnp.einsum('gmxcf,xfd->gmxcd', hidden, down_weight, preferred_element_typ...  56.6 us
    all_to_all x4, starting transfers between devices, experts_layer(): lax.all_to_all(outgoing, 'expert', split_axis=0, concat_axis=0, tiled=True)  14.8 us
    all_to_all x4, starting transfers between devices, experts_layer(): lax.all_to_all(produced, 'expert', split_axis=0, concat_axis=0, tiled=True)  14.3 us
    all_to_all x4, waiting for transfers between devices, experts_layer(): lax.all_to_all(produced, 'expert', split_axis=0, concat_axis=0, tiled=True)  14.2 us
    gather x8, local copies, waits for them, and re-layouts, experts_layer(): flat_tokens[jnp.maximum(source_index, 0)]  9.73 us
  transfers between devices with their start and end apart: 11, of which 6 were waited for; matrix products, arithmetic and copies ran while one was open for 18% of the time, Pallas kernels for 0%

commit v1 on v0

--- a/solution.py
+++ b/solution.py
@@ -6,6 +6,10 @@
 MB = 2
 TICKS = 2
 TOP = 4
+
+
+def handle_gates_on_mesh(raw):
+    return jnp.sum(lax.all_gather(raw, axis_name="dp"), axis=0)
 
 
 def shifted(block, axis, distance):
@@ -60,7 +64,7 @@
         "gmxcd,xdf->gmxcf", arrived, up_weight, preferred_element_type=jnp.float32
     )
     rounded = lax.optimization_barrier(partial_value.astype(jnp.bfloat16)).astype(jnp.float32)
-    summed = lax.psum(rounded.astype(jnp.bfloat16), "dp").astype(jnp.float32)
+    summed = handle_gates_on_mesh(rounded.astype(jnp.bfloat16)).astype(jnp.float32)
     hidden = jax.nn.silu(summed).astype(jnp.bfloat16)
     produced = jnp.einsum(
         "gmxcf,xfd->gmxcd", hidden, down_weight, preferred_element_type=jnp.float32

time: 425 us -> 513 us (1.21)
  blocking collectives: 0 us -> 49 us
  waiting for transfers between devices: 217 us -> 265 us
  starting transfers between devices: 31.2 us -> 15.7 us
  other arithmetic: 5.76 us -> 19 us
    all_gather x0 -> x4, waiting for transfers between devices: none -> 249 us  [handle_gates_on_mesh(): return jnp.sum(lax.all_gather(raw, axis_name='dp'), axis=0)]
    psum x2 -> x0, waiting for transfers between devices: 196 us -> none  [experts_layer(): summed = lax.psum(rounded.astype(jnp.bfloat16), 'dp').astype(jnp.float32)]
    all_to_all x0 -> x4, blocking collectives: none -> 49 us  [experts_layer(): lax.all_to_all(outgoing, 'expert', split_axis=0, concat_axis=0, tiled=True)]
    all_to_all x4 -> x0, starting transfers between devices: 14.8 us -> none  [experts_layer(): lax.all_to_all(outgoing, 'expert', split_axis=0, concat_axis=0, tiled=True)]
    reduce_sum x0 -> x4, other arithmetic: none -> 13.2 us  [handle_gates_on_mesh(): return jnp.sum(lax.all_gather(raw, axis_name='dp'), axis=0)]
    all_to_all x4 -> x0, waiting for transfers between devices: 6.38 us -> none  [experts_layer(): lax.all_to_all(outgoing, 'expert', split_axis=0, concat_axis=0, tiled=True)]
  transfers between devices with their start and end apart: 11 -> 9, of which waited for: 6 -> 6; matrix products, arithmetic and copies ran while one was open for 18% -> 23% of each run, Pallas kernels for 0% -> 0%
where the time goes in v1:
time: 513 us; the launch traced here: 506 us
  waiting for transfers between devices  265 us (52%)
  matrix products  111 us (22%)
  blocking collectives  49 us (10%)
  local copies, waits for them, and re-layouts  31.8 us (6%)
  other arithmetic  19 us (4%)
  starting transfers between devices  15.7 us (3%)
  between operations  14.1 us (3%)
    all_gather x4, waiting for transfers between devices, handle_gates_on_mesh(): return jnp.sum(lax.all_gather(raw, axis_name='dp'), axis=0)  249 us
    dot_general x4, matrix products, experts_layer(): jnp.einsum('gmxcd,xdf->gmxcf', arrived, up_weight, preferred_element_type...  57.2 us
    dot_general x4, matrix products, experts_layer(): jnp.einsum('gmxcf,xfd->gmxcd', hidden, down_weight, preferred_element_typ...  52.6 us
    all_to_all x4, blocking collectives, experts_layer(): lax.all_to_all(outgoing, 'expert', split_axis=0, concat_axis=0, tiled=True)  49 us
    all_to_all x4, waiting for transfers between devices, experts_layer(): lax.all_to_all(produced, 'expert', split_axis=0, concat_axis=0, tiled=True)  16.1 us
    all_to_all x4, starting transfers between devices, experts_layer(): lax.all_to_all(produced, 'expert', split_axis=0, concat_axis=0, tiled=True)  14.1 us
    reduce_sum x4, other arithmetic, handle_gates_on_mesh(): return jnp.sum(lax.all_gather(raw, axis_name='dp'), axis=0)  13.2 us
  transfers between devices with their start and end apart: 9, of which 6 were waited for; matrix products, arithmetic and copies ran while one was open for 23% of the time, Pallas kernels for 0%

profile of v1, /device:TPU:0, one launch (start us, length us, event | category | flops | bytes accessed | tf_op | source)
XLA Modules:
  0.0 506.1 jit_solution(11330180440805573082)
XLA Ops:
  6.5 0.7 fusion.143
  7.6 0.6 reduce-window.30
  8.9 1.4 scatter_custom_fusion.1
  10.3 1.0 slice_bitcast_fusion.1
  11.3 2.3 gather_fusion.2
  14.2 13.8 %all_to_all.40 = bf16[2,1,16,12,896]{4,2,3,1,0:T(8,128)(2,1)S(1)} all-to-all(bf16[2,1,16,12,896]{4,2,3,1,0:T(8,128)(2,1)S(1)} %copy.54), channel_id=1, replica_groups=mesh['section'=4,'expert'=2,'dp'=4] {'expert'}, dimensions={0} | all-to-all | bytes 1376256 | tf_op jit(solution)/shard_map/all_to_all | solution.py:62
  28.0 14.3 %fusion.34 = bf16[2,1,16,12,1152]{4,3,0,2,1:T(8,128)(2,1)} fusion(bf16[1,16,896,1152]{3,2,1,0:T(8,128)(2,1)} %param.8, bf16[2,1,16,12,896]{4,2,3,1,0:T(8,128)(2,1)S(1)} %all_to_all.40), kind=kOutput, calls=%fused_computation.42 | convolution fusion | flops 793165824 | bytes 34603008 | tf_op jit(solution)/shard_map/gmxcd,xdf->gmxcf/dot_general | solution.py:63
  42.6 0.6 reduce-window.26
  43.8 1.4 scatter_custom_fusion
  45.2 2.3 gather_fusion
  48.2 11.7 %all_to_all.41 = bf16[2,1,16,12,896]{4,2,3,1,0:T(8,128)(2,1)S(1)} all-to-all(bf16[2,1,16,12,896]{4,2,3,1,0:T(8,128)(2,1)S(1)} %copy.45), channel_id=1, replica_groups=mesh['section'=4,'expert'=2,'dp'=4] {'expert'}, dimensions={0} | all-to-all | bytes 1376256 | tf_op jit(solution)/shard_map/all_to_all | solution.py:62
  59.8 14.4 %fusion.37 = bf16[2,1,16,12,1152]{4,3,0,2,1:T(8,128)(2,1)} fusion(bf16[1,16,896,1152]{3,2,1,0:T(8,128)(2,1)} %param.8, bf16[2,1,16,12,896]{4,2,3,1,0:T(8,128)(2,1)S(1)} %all_to_all.41), kind=kOutput, calls=%fused_computation.43 | convolution fusion | flops 793165824 | bytes 34603008 | tf_op jit(solution)/shard_map/gmxcd,xdf->gmxcf/dot_general | solution.py:63
  75.9 56.3 %all-gather.11.cloned.1.call-done = bf16[8,1,16,12,1152]{4,3,0,2,1:T(8,128)(2,1)} async-done(((bf16[2,1,16,12,1152]{4,3,0,2,1:T(8,128)(2,1)}), bf16[8,1,16,12,1152]{4,3,0,2,1:T(8,128)(2,1)}) %all-gather.11.cloned.1.call-update) | async-done | bytes 3538960 | tf_op jit(solution)/shard_map/all_gather | solution.py:12
  132.2 3.3 reduce.17
  135.5 13.7 %fusion.74 = bf16[2,1,16,12,896]{4,3,0,2,1:T(8,128)(2,1)S(1)} fusion(bf16[1,16,1152,896]{3,2,1,0:T(8,128)(2,1)} %param.9, bf16[2,16,12,1152]{3,2,0,1:T(8,128)(2,1)S(1)} %reduce.17), kind=kOutput, calls=%fused_computation.66 | convolution fusion | flops 795721728 | bytes 34603008 | tf_op jit(solution)/shard_map/gmxcf,xfd->gmxcd/dot_general | solution.py:69
  149.3 1.1 copy.56
  150.3 3.5 all-to-all-start.3
  153.9 67.8 %all-gather.9.cloned.1.call-done = bf16[8,1,16,12,1152]{4,3,0,2,1:T(8,128)(2,1)} async-done(((bf16[2,1,16,12,1152]{4,3,0,2,1:T(8,128)(2,1)}), bf16[8,1,16,12,1152]{4,3,0,2,1:T(8,128)(2,1)}) %all-gather.9.cloned.1.call-update) | async-done | bytes 3538960 | tf_op jit(solution)/shard_map/all_gather | solution.py:12
  221.6 3.3 reduce.16
  224.9 12.5 %fusion.77 = bf16[2,1,16,12,896]{4,3,0,2,1:T(8,128)(2,1)S(1)} fusion(bf16[1,16,1152,896]{3,2,1,0:T(8,128)(2,1)} %param.9, bf16[2,16,12,1152]{3,2,0,1:T(8,128)(2,1)S(1)} %reduce.16), kind=kOutput, calls=%fused_computation.67 | convolution fusion | flops 795721728 | bytes 34603008 | tf_op jit(solution)/shard_map/gmxcf,xfd->gmxcd/dot_general | solution.py:69
  237.5 1.1 copy.47
  238.5 3.5 all-to-all-start.1
  242.8 1.2 gather_fusion.3
  244.1 8.0 %all-to-all-done.1 = bf16[2,1,16,12,896]{4,2,3,1,0:T(8,128)(2,1)S(1)} async-done(((bf16[2,1,16,12,896]{4,2,3,1,0:T(8,128)(2,1)}), bf16[2,1,16,12,896]{4,2,3,1,0:T(8,128)(2,1)S(1)}, u32[]{:S(2)}, u32[]{:S(2)}) %all-to-all-start.1) | async-done | bytes 688160 | tf_op jit(solution)/shard_map/all_to_all | solution.py:72
  252.5 1.2 gather_fusion.1
  254.7 1.5 collective-permute-start
  256.2 1.4 scatter_custom_fusion.3
  257.9 2.3 gather_fusion.6
  260.7 11.1 %all_to_all.42 = bf16[2,1,16,12,896]{4,2,3,1,0:T(8,128)(2,1)S(1)} all-to-all(bf16[2,1,16,12,896]{4,2,3,1,0:T(8,128)(2,1)S(1)} %copy.72), channel_id=1, replica_groups=mesh['section'=4,'expert'=2,'dp'=4] {'expert'}, dimensions={0} | all-to-all | bytes 1376256 | tf_op jit(solution)/shard_map/all_to_all | solution.py:62
  271.8 14.3 %fusion.28 = bf16[2,1,16,12,1152]{4,3,0,2,1:T(8,128)(2,1)} fusion(bf16[1,16,896,1152]{3,2,1,0:T(8,128)(2,1)} %param.8, bf16[2,1,16,12,896]{4,2,3,1,0:T(8,128)(2,1)S(1)} %all_to_all.42), kind=kOutput, calls=%fused_computation.40 | convolution fusion | flops 793165824 | bytes 34603008 | tf_op jit(solution)/shard_map/gmxcd,xdf->gmxcf/dot_general | solution.py:63
  287.6 1.4 scatter_custom_fusion.2
  289.2 2.3 gather_fusion.4
  292.0 12.4 %all_to_all.43 = bf16[2,1,16,12,896]{4,2,3,1,0:T(8,128)(2,1)S(1)} all-to-all(bf16[2,1,16,12,896]{4,2,3,1,0:T(8,128)(2,1)S(1)} %copy.63), channel_id=1, replica_groups=mesh['section'=4,'expert'=2,'dp'=4] {'expert'}, dimensions={0} | all-to-all | bytes 1376256 | tf_op jit(solution)/shard_map/all_to_all | solution.py:62
  304.4 14.3 %fusion.31 = bf16[2,1,16,12,1152]{4,3,0,2,1:T(8,128)(2,1)} fusion(bf16[1,16,896,1152]{3,2,1,0:T(8,128)(2,1)} %param.8, bf16[2,1,16,12,896]{4,2,3,1,0:T(8,128)(2,1)S(1)} %all_to_all.43), kind=kOutput, calls=%fused_computation.41 | convolution fusion | flops 793165824 | bytes 34603008 | tf_op jit(solution)/shard_map/gmxcd,xdf->gmxcf/dot_general | solution.py:63
  318.9 57.3 %all-gather.15.cloned.1.call-done = bf16[8,1,16,12,1152]{4,3,0,2,1:T(8,128)(2,1)} async-done(((bf16[2,1,16,12,1152]{4,3,0,2,1:T(8,128)(2,1)}), bf16[8,1,16,12,1152]{4,3,0,2,1:T(8,128)(2,1)}) %all-gather.15.cloned.1.call-update) | async-done | bytes 3538960 | tf_op jit(solution)/shard_map/all_gather | solution.py:12
  376.2 3.3 reduce.19
  379.5 13.7 %fusion.68 = bf16[2,1,16,12,896]{4,3,0,2,1:T(8,128)(2,1)S(1)} fusion(bf16[1,16,1152,896]{3,2,1,0:T(8,128)(2,1)} %param.9, bf16[2,16,12,1152]{3,2,0,1:T(8,128)(2,1)S(1)} %reduce.19), kind=kOutput, calls=%fused_computation.64 | convolution fusion | flops 795721728 | bytes 34603008 | tf_op jit(solution)/shard_map/gmxcf,xfd->gmxcd/dot_general | solution.py:69
  393.2 1.1 copy.74
  394.3 3.5 all-to-all-start.7
  397.8 67.6 %all-gather.13.cloned.1.call-done = bf16[8,1,16,12,1152]{4,3,0,2,1:T(8,128)(2,1)} async-done(((bf16[2,1,16,12,1152]{4,3,0,2,1:T(8,128)(2,1)}), bf16[8,1,16,12,1152]{4,3,0,2,1:T(8,128)(2,1)}) %all-gather.13.cloned.1.call-update) | async-done | bytes 3538960 | tf_op jit(solution)/shard_map/all_gather | solution.py:12
  465.5 3.3 reduce.18
  468.8 12.5 %fusion.71 = bf16[2,1,16,12,896]{4,3,0,2,1:T(8,128)(2,1)S(1)} fusion(bf16[1,16,1152,896]{3,2,1,0:T(8,128)(2,1)} %param.9, bf16[2,16,12,1152]{3,2,0,1:T(8,128)(2,1)S(1)} %reduce.18), kind=kOutput, calls=%fused_computation.65 | convolution fusion | flops 795721728 | bytes 34603008 | tf_op jit(solution)/shard_map/gmxcf,xfd->gmxcd/dot_general | solution.py:69
  481.3 1.1 copy.65
  482.4 3.5 all-to-all-start.5
  486.6 1.2 gather_fusion.7
  487.9 8.1 %all-to-all-done.5 = bf16[2,1,16,12,896]{4,2,3,1,0:T(8,128)(2,1)S(1)} async-done(((bf16[2,1,16,12,896]{4,2,3,1,0:T(8,128)(2,1)}), bf16[2,1,16,12,896]{4,2,3,1,0:T(8,128)(2,1)S(1)}, u32[]{:S(2)}, u32[]{:S(2)}) %all-to-all-start.5) | async-done | bytes 688160 | tf_op jit(solution)/shard_map/all_to_all | solution.py:72
  496.3 1.2 gather_fusion.5
  498.5 0.8 maximum_bitcast_fusion
  (141 shorter events, 11.9 us)
Async XLA Ops:
  6.5 125.7 %all-gather.11.cloned.1.call-start = ((), (), s32[]{:S(2)}) async-start(), calls=%async_computation.9 | async-start | bytes 5898240 | tf_op jit(solution)/shard_map/all_gather | solution.py:12
  42.3 179.4 %all-gather.9.cloned.1.call-start = ((), (), s32[]{:S(2)}) async-start(), calls=%async_computation.8 | async-start | bytes 5898240 | tf_op jit(solution)/shard_map/all_gather | solution.py:12
  59.8 15.9 %copy-start.2 = (f32[2,1,2,64,4]{3,4,2,1,0:T(4,128)S(1)}, f32[2,1,2,64,4]{3,4,2,1,0:T(4,128)}, u32[]{:S(2)}) copy-start(f32[2,1,2,64,4]{3,4,2,1,0:T(4,128)} %param.11) | copy-start | bytes 12292
  150.3 88.2 %all-to-all-start.3 = ((bf16[2,1,16,12,896]{4,2,3,1,0:T(8,128)(2,1)}), bf16[2,1,16,12,896]{4,2,3,1,0:T(8,128)(2,1)S(1)}, u32[]{:S(2)}, u32[]{:S(2)}) async-start(bf16[2,1,16,12,896]{4,2,3,1,0:T(8,128)(2,1)} %copy.56), calls=%async_computation.3 | async-start | bytes 1376256 | tf_op jit(solution)/shard_map/all_to_all | solution.py:72
  238.5 13.6 %all-to-all-start.1 = ((bf16[2,1,16,12,896]{4,2,3,1,0:T(8,128)(2,1)}), bf16[2,1,16,12,896]{4,2,3,1,0:T(8,128)(2,1)S(1)}, u32[]{:S(2)}, u32[]{:S(2)}) async-start(bf16[2,1,16,12,896]{4,2,3,1,0:T(8,128)(2,1)} %copy.47), calls=%async_computation.1 | async-start | bytes 1376256 | tf_op jit(solution)/shard_map/all_to_all | solution.py:72
  242.1 134.1 %all-gather.15.cloned.1.call-start = ((), (), s32[]{:S(2)}) async-start(), calls=%async_computation.11 | async-start | bytes 5898240 | tf_op jit(solution)/shard_map/all_gather | solution.py:12
  253.7 1.0 copy-start
  253.7 4.2 copy-start.1
  254.7 3.1 collective-permute-start
  286.1 179.4 %all-gather.13.cloned.1.call-start = ((), (), s32[]{:S(2)}) async-start(), calls=%async_computation.10 | async-start | bytes 5898240 | tf_op jit(solution)/shard_map/all_gather | solution.py:12
  394.3 88.1 %all-to-all-start.7 = ((bf16[2,1,16,12,896]{4,2,3,1,0:T(8,128)(2,1)}), bf16[2,1,16,12,896]{4,2,3,1,0:T(8,128)(2,1)S(1)}, u32[]{:S(2)}, u32[]{:S(2)}) async-start(bf16[2,1,16,12,896]{4,2,3,1,0:T(8,128)(2,1)} %copy.74), calls=%async_computation.7 | async-start | bytes 1376256 | tf_op jit(solution)/shard_map/all_to_all | solution.py:72
  482.4 13.6 %all-to-all-start.5 = ((bf16[2,1,16,12,896]{4,2,3,1,0:T(8,128)(2,1)}), bf16[2,1,16,12,896]{4,2,3,1,0:T(8,128)(2,1)S(1)}, u32[]{:S(2)}, u32[]{:S(2)}) async-start(bf16[2,1,16,12,896]{4,2,3,1,0:T(8,128)(2,1)} %copy.65), calls=%async_computation.5 | async-start | bytes 1376256 | tf_op jit(solution)/shard_map/all_to_all | solution.py:72
Sparse Core Ops, SparseCore 0:
  42.4 89.7 all-gather.10
  133.8 87.8 all-gather.8
  286.2 89.9 all-gather.14
  377.6 87.8 all-gather.12
